TPU v7x, 512 devices: a whole 4x4x16 slice. The times are simulated.
512 devices in a mesh: row: 32 (over z, core), col: 16 (over x, y).
Axes of the slice: x: 4, y: 4, z: 16, core: 2. Of those that a mesh axis runs over, the one named last changes fastest.
Arguments:
- tensor: float32 [16, 8192, 4096], P(None, 'row', 'col'), may hold values from -270 to 270
- factor_b: float32 [64, 4096], P(None, 'col'), may hold values from -6 to 6
- factor_c: float32 [16, 64], replicated, may hold values from -6 to 6
Outputs:
- result_a: float32 [64, 8192], P(None, 'row')
- result_b: float32 [64, 4096], P(None, 'col')
- column_scales: float32 [2, 64], replicated
All inputs are finite; a program needn't handle non-finite values.
Results may differ from a plain program's by a relative error of at most 0.0003.
Values sent between devices are 32-bit elements; how exact they have to be, the bound alone decides.
A program may use at most 64 MiB of HBM per device.

v0:
```python
import jax
import jax.numpy as jnp
from jax import lax
from jax.sharding import PartitionSpec as P

SWEEPS = 3


epsilon = 1e-06


def gram_of(factor):
    return jnp.dot(
        factor, factor.T, precision=lax.Precision.HIGHEST, preferred_element_type=jnp.float32
    )


def settle_left(solved, count):
    squares = lax.psum(jnp.sum(solved * solved, axis=1), "row")
    scales = jnp.sqrt(squares / count + epsilon)
    normed = solved / scales[:, None]
    return (normed, scales, lax.psum(gram_of(normed), "row"))


def settle_right(solved, count):
    squares = lax.psum(jnp.sum(solved * solved, axis=1), "col")
    scales = jnp.sqrt(squares / count + epsilon)
    normed = solved / scales[:, None]
    return (normed, scales, lax.psum(gram_of(normed), "col"))


def shards(tensor, factor_b, factor_c):
    highest = lax.Precision.HIGHEST
    rows_all = tensor.shape[1] * lax.axis_size("row")
    cols_all = tensor.shape[2] * lax.axis_size("col")
    rank = factor_c.shape[1]
    identity = jnp.eye(rank, dtype=jnp.float32)
    gram_c = jnp.dot(factor_c.T, factor_c, precision=highest, preferred_element_type=jnp.float32)
    current_b = factor_b
    gram_b = lax.psum(gram_of(current_b), "col")
    current_a = jnp.zeros((rank, tensor.shape[1]), jnp.float32)
    scales_a = jnp.zeros((rank,), jnp.float32)
    scales_b = jnp.zeros((rank,), jnp.float32)
    for sweep in range(SWEEPS):
        lower_a = jnp.linalg.cholesky(gram_c * gram_b + cols_all * identity)
        inner = jnp.einsum("kij,rj->kir", tensor, current_b, precision=highest)
        partial_a = jnp.einsum("kir,kr->ri", inner, factor_c, precision=highest)
        summed_a = lax.psum(partial_a, "col")
        solved_a = jax.scipy.linalg.cho_solve((lower_a, True), summed_a)
        current_a, scales_a, gram_a = settle_left(solved_a, rows_all)
        lower_b = jnp.linalg.cholesky(gram_c * gram_a + rows_all * identity)
        outer = jnp.einsum("ri,kij->krj", current_a, tensor, precision=highest)
        partial_b = jnp.einsum("krj,kr->rj", outer, factor_c, precision=highest)
        summed_b = lax.psum(partial_b, "row")
        solved_b = jax.scipy.linalg.cho_solve((lower_b, True), summed_b)
        current_b, scales_b, gram_b = settle_right(solved_b, cols_all)
    return (current_a, current_b, jnp.stack([scales_a, scales_b]))


def solution(mesh):
    in_specs = (P(None, "row", "col"), P(None, "col"), P())
    out_specs = (P(None, "row"), P(None, "col"), P())
    return jax.shard_map(shards, mesh=mesh, in_specs=in_specs, out_specs=out_specs, check_vma=False)
```

profile of v0, /device:TPU:1, one launch (start us, length us, event | category | flops | bytes accessed | tf_op | source)
XLA Modules:
  0.0 1629.8 jit_solution(3930097045022969631)
XLA Ops:
  14.6 61.6 %psum.126 = f32[64,64]{0,1:T(8,128)S(1)} all-reduce(f32[64,64]{0,1:T(8,128)S(1)} %fusion.76), channel_id=1, replica_groups=mesh['row'=32,'col'=16] {'col'}, use_global_device_ids=true, to_apply=%region_0.0 | all-reduce | flops 4096 | bytes 32768 | tf_op jit(solution)/shard_map/psum | solution.py:40
  76.6 5.8 cholesky.104
  88.8 41.6 %all-reduce.7.cloned.1.call-done = f32[64,256]{1,0:T(8,128)} async-done(((f32[64,256]{1,0:T(8,128)}), f32[64,256]{1,0:T(8,128)}) %all-reduce.7.cloned.1.call-update) | async-done | bytes 65552 | tf_op jit(solution)/shard_map/psum | solution.py:48
  131.7 48.6 %psum.128 = f32[64]{0:T(128)S(1)} all-reduce(f32[64]{0:T(128)S(1)} %get-tuple-element.11), channel_id=1, replica_groups=mesh['row'=32,'col'=16] {'row'}, use_global_device_ids=true, to_apply=%region_5.0 | all-reduce | flops 64 | bytes 512 | tf_op jit(solution)/shard_map/psum | solution.py:19
  185.4 87.8 %psum.129 = f32[64,64]{0,1:T(8,128)S(1)} all-reduce(f32[64,64]{0,1:T(8,128)S(1)} %fusion.70), channel_id=1, replica_groups=mesh['row'=32,'col'=16] {'row'}, use_global_device_ids=true, to_apply=%region_6.0 | all-reduce | flops 4096 | bytes 32768 | tf_op jit(solution)/shard_map/psum | solution.py:22
  273.4 5.8 cholesky.115
  287.9 178.0 %all-reduce.9.cloned.1.call-done = f32[64,256]{1,0:T(8,128)} async-done(((f32[64,256]{1,0:T(8,128)}), f32[64,256]{1,0:T(8,128)}) %all-reduce.9.cloned.1.call-update) | async-done | bytes 65552 | tf_op jit(solution)/shard_map/psum | solution.py:54
  467.3 33.1 %psum.131 = f32[64]{0:T(128)S(1)} all-reduce(f32[64]{0:T(128)S(1)} %get-tuple-element.13), channel_id=1, replica_groups=mesh['row'=32,'col'=16] {'col'}, use_global_device_ids=true, to_apply=%region_9.0 | all-reduce | flops 64 | bytes 512 | tf_op jit(solution)/shard_map/psum | solution.py:26
  500.7 6.3 fusion.21
  507.0 56.0 %psum.132 = f32[64,64]{0,1:T(8,128)S(1)} all-reduce(f32[64,64]{0,1:T(8,128)S(1)} %fusion.71), channel_id=1, replica_groups=mesh['row'=32,'col'=16] {'col'}, use_global_device_ids=true, to_apply=%region_10.0 | all-reduce | flops 4096 | bytes 32768 | tf_op jit(solution)/shard_map/psum | solution.py:29
  577.2 113.5 %all-reduce.11.cloned.1.call-done = f32[64,256]{1,0:T(8,128)} async-done(((f32[64,256]{1,0:T(8,128)}), f32[64,256]{1,0:T(8,128)}) %all-reduce.11.cloned.1.call-update) | async-done | bytes 65552 | tf_op jit(solution)/shard_map/psum | solution.py:48
  692.0 48.6 %psum.134 = f32[64]{0:T(128)S(1)} all-reduce(f32[64]{0:T(128)S(1)} %get-tuple-element.15), channel_id=1, replica_groups=mesh['row'=32,'col'=16] {'row'}, use_global_device_ids=true, to_apply=%region_13.0 | all-reduce | flops 64 | bytes 512 | tf_op jit(solution)/shard_map/psum | solution.py:19
  745.8 88.0 %psum.135 = f32[64,64]{0,1:T(8,128)S(1)} all-reduce(f32[64,64]{0,1:T(8,128)S(1)} %fusion.72), channel_id=1, replica_groups=mesh['row'=32,'col'=16] {'row'}, use_global_device_ids=true, to_apply=%region_14.0 | all-reduce | flops 4096 | bytes 32768 | tf_op jit(solution)/shard_map/psum | solution.py:22
  833.9 5.8 cholesky.137
  848.0 178.4 %all-reduce.13.cloned.1.call-done = f32[64,256]{1,0:T(8,128)} async-done(((f32[64,256]{1,0:T(8,128)}), f32[64,256]{1,0:T(8,128)}) %all-reduce.13.cloned.1.call-update) | async-done | bytes 65552 | tf_op jit(solution)/shard_map/psum | solution.py:54
  1027.8 33.1 %psum.137 = f32[64]{0:T(128)S(1)} all-reduce(f32[64]{0:T(128)S(1)} %get-tuple-element.17), channel_id=1, replica_groups=mesh['row'=32,'col'=16] {'col'}, use_global_device_ids=true, to_apply=%region_17.0 | all-reduce | flops 64 | bytes 512 | tf_op jit(solution)/shard_map/psum | solution.py:26
  1061.2 6.3 fusion.17
  1067.5 56.0 %psum.138 = f32[64,64]{0,1:T(8,128)S(1)} all-reduce(f32[64,64]{0,1:T(8,128)S(1)} %fusion.73), channel_id=1, replica_groups=mesh['row'=32,'col'=16] {'col'}, use_global_device_ids=true, to_apply=%region_18.0 | all-reduce | flops 4096 | bytes 32768 | tf_op jit(solution)/shard_map/psum | solution.py:29
  1123.6 5.8 cholesky.148
  1137.7 113.5 %all-reduce.15.cloned.1.call-done = f32[64,256]{1,0:T(8,128)} async-done(((f32[64,256]{1,0:T(8,128)}), f32[64,256]{1,0:T(8,128)}) %all-reduce.15.cloned.1.call-update) | async-done | bytes 65552 | tf_op jit(solution)/shard_map/psum | solution.py:48
  1252.5 48.8 %psum.140 = f32[64]{0:T(128)S(1)} all-reduce(f32[64]{0:T(128)S(1)} %get-tuple-element.19), channel_id=1, replica_groups=mesh['row'=32,'col'=16] {'row'}, use_global_device_ids=true, to_apply=%region_21.0 | all-reduce | flops 64 | bytes 512 | tf_op jit(solution)/shard_map/psum | solution.py:19
  1306.5 87.8 %psum.141 = f32[64,64]{0,1:T(8,128)S(1)} all-reduce(f32[64,64]{0,1:T(8,128)S(1)} %fusion.77), channel_id=1, replica_groups=mesh['row'=32,'col'=16] {'row'}, use_global_device_ids=true, to_apply=%region_22.0 | all-reduce | flops 4096 | bytes 32768 | tf_op jit(solution)/shard_map/psum | solution.py:22
  1408.5 178.5 %all-reduce.17.cloned.1.call-done = f32[64,256]{1,0:T(8,128)} async-done(((f32[64,256]{1,0:T(8,128)}), f32[64,256]{1,0:T(8,128)}) %all-reduce.17.cloned.1.call-update) | async-done | bytes 65552 | tf_op jit(solution)/shard_map/psum | solution.py:54
  1588.3 33.1 %psum.143 = f32[64]{0:T(128)S(1)} all-reduce(f32[64]{0:T(128)S(1)} %get-tuple-element.21), channel_id=1, replica_groups=mesh['row'=32,'col'=16] {'col'}, use_global_device_ids=true, to_apply=%region_25.28 | all-reduce | flops 64 | bytes 512 | tf_op jit(solution)/shard_map/psum | solution.py:26
  (105 shorter events, 93.2 us)
Async XLA Ops:
  7.2 0.8 copy-start
  7.2 69.1 %copy-start.2 = (f32[16,64]{1,0:T(8,128)S(1)}, f32[16,64]{1,0:T(8,128)}, u32[]{:S(2)}) copy-start(f32[16,64]{1,0:T(8,128)} %param.8) | copy-start | bytes 12292
  7.2 123.1 %all-reduce.7.cloned.1.call-start = ((), (), s32[]{:S(2)}) async-start(), calls=%async_computation | async-start | bytes 131072 | tf_op jit(solution)/shard_map/psum | solution.py:48
  14.4 451.5 %all-reduce.9.cloned.1.call-start = ((), (), s32[]{:S(2)}) async-start(), calls=%async_computation.1 | async-start | bytes 131072 | tf_op jit(solution)/shard_map/psum | solution.py:54
  281.9 408.8 %all-reduce.11.cloned.1.call-start = ((), (), s32[]{:S(2)}) async-start(), calls=%async_computation.2 | async-start | bytes 131072 | tf_op jit(solution)/shard_map/psum | solution.py:48
  571.6 454.8 %all-reduce.13.cloned.1.call-start = ((), (), s32[]{:S(2)}) async-start(), calls=%async_computation.3 | async-start | bytes 131072 | tf_op jit(solution)/shard_map/psum | solution.py:54
  842.4 408.8 %all-reduce.15.cloned.1.call-start = ((), (), s32[]{:S(2)}) async-start(), calls=%async_computation.4 | async-start | bytes 131072 | tf_op jit(solution)/shard_map/psum | solution.py:48
  1132.1 454.9 %all-reduce.17.cloned.1.call-start = ((), (), s32[]{:S(2)}) async-start(), calls=%async_computation.5 | async-start | bytes 131072 | tf_op jit(solution)/shard_map/psum | solution.py:54
  1301.4 321.3 %copy-start.1 = (f32[64,256]{1,0:T(8,128)}, f32[64,256]{1,0:T(8,128)S(1)}, u32[]{:S(2)}) copy-start(f32[64,256]{1,0:T(8,128)S(1)} %broadcast_divide_fusion.1) | copy-start | bytes 196612
Sparse Core Ops, SparseCore 0:
  14.5 115.7 all-reduce.6
  282.0 183.8 all-reduce.8
  571.7 118.9 all-reduce.10
  842.5 183.8 all-reduce.12
  1132.2 118.9 all-reduce.14
  1403.0 183.8 all-reduce.16
where the time goes:
time: 1640 us; the launch traced here: 1630 us
  waiting for transfers between devices  803 us (49%)
  blocking collectives  683 us (42%)
  other arithmetic  74 us (5%)
  matrix products  49.1 us (3%)
    psum x3, waiting for transfers between devices, shards(): summed_b = lax.psum(partial_b, 'row')  535 us
    psum x3, waiting for transfers between devices, shards(): summed_a = lax.psum(partial_a, 'col')  268 us
    psum x3, blocking collectives, settle_left(): return (normed, scales, lax.psum(gram_of(normed), 'row'))  264 us
    psum x3, blocking collectives, settle_left(): squares = lax.psum(jnp.sum(solved * solved, axis=1), 'row')  146 us
    psum x2, blocking collectives, settle_right(): return (normed, scales, lax.psum(gram_of(normed), 'col'))  112 us
    psum x3, blocking collectives, settle_right(): squares = lax.psum(jnp.sum(solved * solved, axis=1), 'col')  99.4 us
    psum x1, blocking collectives, shards(): gram_b = lax.psum(gram_of(current_b), 'col')  61.6 us
  transfers between devices with their start and end apart: 6, of which 6 were waited for; matrix products, arithmetic and copies ran while one was open for 2% of the time, Pallas kernels for 0%

commit v1 on v0

v1 whole, which is shorter than its diff:
```python
import jax
import jax.numpy as jnp
from jax import lax
from jax.experimental import pallas as pl
from jax.experimental.pallas import tpu as pltpu
from jax.sharding import PartitionSpec as P

SWEEPS = 3
EPSILON = 1e-06
MESH = pl.DeviceIdType.MESH
HIGHEST = lax.Precision.HIGHEST
F32 = jnp.float32
BF16 = jnp.bfloat16

CHIPS = 16
COLS = 16
SIDE = 4

SERVED = ((0, 0), (1, 0), (3, 0), (0, 1), (0, 3), (2, 0), (1, 1), (1, 3))
WINDOW = (-4, -3, 3, -2, 2, -1, 1, 0)


def ring(offset, size):
    return min(offset % size, -offset % size)


def halves(x):
    high = x.astype(BF16)
    return high, (x - high.astype(F32)).astype(BF16)


def stacked(x):
    return jnp.concatenate(halves(x), axis=0)


def gram_of(factor):
    return lax.dot_general(factor, factor, (((1,), (1,)), ((), ())), precision=HIGHEST, preferred_element_type=F32)


def packed(gram):
    return jnp.concatenate([gram[:32], gram[32:]], axis=1)


def unpacked(pack):
    return jnp.concatenate([pack[:, :64], pack[:, 64:]], axis=0)


def spread(row, lanes=128):
    return jnp.broadcast_to(row, (8, lanes))


def eliminate(work):
    rows = [work[8 * i : 8 * i + 8] for i in range(8)]
    sublane = lax.broadcasted_iota(jnp.int32, (8, 128), 0)
    for panel in range(8):
        columns = [
            [jnp.broadcast_to(rows[i][:, 8 * panel + k : 8 * panel + k + 1], (8, 128)) for k in range(8)]
            for i in range(8)
        ]
        own = list(columns[panel])
        value = rows[panel]
        inverses = jnp.zeros((8, 128), F32)
        for k in range(8):
            inverse = 1.0 / spread(own[k][k : k + 1])
            inverses = jnp.where(sublane == k, inverse, inverses)
            factor = jnp.where(sublane == k, 0.0, own[k] * inverse)
            value = value - factor * spread(value[k : k + 1])
            for m in range(k + 1, 8):
                own[m] = own[m] - factor * spread(own[m][k : k + 1])
        value = value * inverses
        rows[panel] = value
        pivots = [spread(value[k : k + 1]) for k in range(8)]
        for i in range(8):
            if i != panel:
                total = rows[i]
                for k in range(8):
                    total = total - columns[i][k] * pivots[k]
                rows[i] = total
    return jnp.concatenate(rows, axis=0)[:, 64:]


def kernel(
    tensor, factor_b, factor_c,
    out_a, out_b, out_scales,
    staged, high, low, wide_c, twin_c, gram_c, solved_a, solved_b,
    part_a, sums_a, full_a, grams_a,
    part_b, pair_b, half_b, sums_b, full_b,
    halves_g, pair_g, grams_b, full_g, squares,
    load_sem, send_sem, recv_sem, last_send, last_recv,
):
    row, col = lax.axis_index("row"), lax.axis_index("col")
    chip, core = row // 2, lax.rem(row, 2)
    col_x, col_y = col // SIDE, lax.rem(col, SIDE)
    sibling = (row + 1 - 2 * core, col)

    def at_col(dx, dy):
        return lax.rem(col_x + dx, SIDE), lax.rem(col_y + dy, SIDE)

    def share_of(x, y):
        return lax.rem(x, 2) * SIDE + lax.rem(y + 2 * (x // 2), SIDE)

    def at_chip(offset):
        return lax.rem(chip + offset + CHIPS, CHIPS)

    col_offsets = [(dx, dy) for dx in range(SIDE) for dy in range(SIDE) if (dx, dy) != (0, 0)]
    col_offsets.sort(key=lambda o: -ring(o[0], SIDE) - ring(o[1], SIDE))
    col_peers = [at_col(*offset) for offset in col_offsets]
    chip_offsets = sorted(range(1, CHIPS), key=lambda o: -ring(o, CHIPS))
    chip_peers = [at_chip(offset) for offset in chip_offsets]
    share = share_of(col_x, col_y)
    tile = lax.rem(chip, 8)

    def device_on_col(x, y):
        return (row, x * SIDE + y)

    def device_on_row(z, c):
        return (z * 2 + c, col)

    barrier = pltpu.get_barrier_semaphore()

    chunks = tensor.shape[0]

    def load(k):
        return pltpu.make_async_copy(tensor.at[k], staged.at[k], load_sem.at[k])

    def start_load(k, carry):
        load(k).start()
        return carry

    lax.fori_loop(0, chunks, start_load, 0)

    greeted = [device_on_col(x, y) for x, y in col_peers]
    greeted += [device_on_row(z, c) for z in chip_peers for c in (0, 1)] + [sibling]
    for device in greeted:
        pl.semaphore_signal(barrier, inc=1, device_id=device, device_id_type=MESH)

    c = factor_c[...]
    gram_c[...] = lax.dot_general(c, c, (((0,), (0,)), ((), ())), precision=HIGHEST, preferred_element_type=F32)
    twin_c[...] = jnp.concatenate([c, c], axis=1)
    c_columns = c.T
    for k in range(chunks):
        wide_c[k] = jnp.broadcast_to(c_columns[:, k : k + 1], (64, 128))
    solved_b[...] = factor_b[...]

    def take(k, carry):
        load(k).wait()
        first, second = halves(staged[k])
        high[k] = first
        low[k] = second
        return carry

    lax.fori_loop(0, chunks, take, 0)

    eye = jnp.where(
        lax.broadcasted_iota(jnp.int32, (64, 64), 0) == lax.broadcasted_iota(jnp.int32, (64, 64), 1), 1.0, 0.0
    ).astype(F32)
    rows_all = 32.0 * tensor.shape[1]
    cols_all = 16.0 * tensor.shape[2]

    def scales_row(gram, count):
        return jnp.sqrt(jnp.sum(gram * eye, axis=0, keepdims=True) / count + EPSILON)

    def scales_column(gram, count):
        return jnp.sqrt(jnp.sum(gram * eye, axis=1, keepdims=True) / count + EPSILON)

    def send(source, target, sweep, kind, device):
        pltpu.make_async_remote_copy(
            src_ref=source, dst_ref=target, send_sem=send_sem.at[sweep, kind], recv_sem=recv_sem.at[sweep, kind],
            device_id=device, device_id_type=MESH,
        ).start()

    def arrived(like, sweep, kind):
        pltpu.make_async_copy(like, like, recv_sem.at[sweep, kind]).wait()

    def left(like, sweep, kind):
        pltpu.make_async_copy(like, like, send_sem.at[sweep, kind]).wait()

    def added(ref, sweep):
        total = ref[sweep, 0]
        for source in range(1, 16):
            total = total + ref[sweep, source]
        return total

    pl.semaphore_wait(barrier, len(greeted))

    def sweep_body(sweep, carry):
        b = solved_b[...]
        grams_a[sweep, col] = packed(gram_of(b))
        for x, y in col_peers:
            send(grams_a.at[sweep, col], grams_a.at[sweep, col], sweep, 0, device_on_col(x, y))
        weights = stacked(b)
        total = jnp.zeros((256, 128), F32)
        for k in range(chunks):
            part = lax.dot_general(high[k], weights, (((1,), (1,)), ((), ())), preferred_element_type=F32)
            part = part + lax.dot_general(low[k], weights, (((1,), (1,)), ((), ())), preferred_element_type=F32)
            total = total + part * twin_c[k : k + 1, :]
        part_a[sweep] = (total[:, :64] + total[:, 64:]).T.reshape(8, 8, 256)
        for x, y in col_peers:
            send(part_a.at[sweep, share_of(x, y)], sums_a.at[sweep, col], sweep, 1, device_on_col(x, y))
        sums_a[sweep, col] = part_a[sweep, share]
        arrived(sums_a.at[sweep, pl.ds(0, 15)], sweep, 1)
        full_a[sweep, share] = added(sums_a, sweep)
        for offset in SERVED[1:]:
            send(full_a.at[sweep, share], full_a.at[sweep, share], sweep, 2, device_on_col(*at_col(*offset)))
        arrived(grams_a.at[sweep, pl.ds(0, 15)], sweep, 0)
        gram = unpacked(added(grams_a, sweep))
        given = sweep == 0
        across = jnp.where(given, 1.0, 1.0 / scales_row(gram, cols_all))
        down = jnp.where(given, 1.0, 1.0 / scales_column(gram, cols_all))
        system = gram_c[...] * (gram * down * across) + cols_all * eye
        solver = eliminate(jnp.concatenate([system, eye * across], axis=1))
        arrived(full_a.at[sweep, pl.ds(0, 7)], sweep, 2)
        a = jnp.dot(solver, full_a[sweep].reshape(64, 256), precision=HIGHEST, preferred_element_type=F32)
        solved_a[...] = a

        halves_g[sweep] = packed(gram_of(a)).reshape(2, 16, 128)
        send(halves_g.at[sweep, 1 - core], pair_g.at[sweep], sweep, 3, sibling)
        total = jnp.zeros((128, 256), F32)
        for k in range(chunks):
            scaled = jnp.concatenate([wide_c[k], wide_c[k]], axis=1) * a
            weights = stacked(scaled)
            total = total + jnp.dot(weights, high[k], preferred_element_type=F32)
            total = total + jnp.dot(weights, low[k], preferred_element_type=F32)
        total = total[:64] + total[64:]
        part_b[sweep, 0] = total[:, :128]
        part_b[sweep, 1] = total[:, 128:]
        send(part_b.at[sweep, 1 - core], pair_b.at[sweep], sweep, 4, sibling)
        arrived(pair_g.at[sweep], sweep, 3)
        grams_b[sweep, chip] = halves_g[sweep, core] + pair_g[sweep]
        for z in chip_peers:
            send(grams_b.at[sweep, chip], grams_b.at[sweep, chip], sweep, 5, device_on_row(z, core))
        arrived(pair_b.at[sweep], sweep, 4)
        half_b[sweep] = (part_b[sweep, core] + pair_b[sweep]).reshape(8, 8, 128)
        for z in chip_peers:
            send(half_b.at[sweep, lax.rem(z, 8)], sums_b.at[sweep, chip], sweep, 6, device_on_row(z, core))
        sums_b[sweep, chip] = half_b[sweep, tile]
        arrived(grams_b.at[sweep, pl.ds(0, 15)], sweep, 5)
        full_g[sweep, core] = added(grams_b, sweep)
        send(full_g.at[sweep, core], full_g.at[sweep, core], sweep, 7, sibling)
        arrived(sums_b.at[sweep, pl.ds(0, 15)], sweep, 6)
        full_b[sweep, core, tile] = added(sums_b, sweep)
        for offset in WINDOW:
            z = at_chip(offset)
            own = full_b.at[sweep, core, tile]
            send(own, own, sweep, 8, device_on_row(z, 1 - core))
            if offset:
                send(own, own, sweep, 8, device_on_row(z, core))
        arrived(pair_g.at[sweep], sweep, 7)
        gram = unpacked(full_g[sweep].reshape(32, 128))
        scales = scales_row(gram, rows_all)
        out_scales[0:1, :] = scales
        across = 1.0 / scales
        down = 1.0 / scales_column(gram, rows_all)
        out_a[...] = a * down
        system = gram_c[...] * (gram * down * across) + rows_all * eye
        solver = eliminate(jnp.concatenate([system, eye * across], axis=1))
        arrived(sums_b.at[sweep, pl.ds(0, 15)], sweep, 8)
        summed = jnp.concatenate([full_b[sweep, 0].reshape(64, 128), full_b[sweep, 1].reshape(64, 128)], axis=1)
        solved_b[...] = jnp.dot(solver, summed, precision=HIGHEST, preferred_element_type=F32)
        return carry

    lax.fori_loop(0, SWEEPS, sweep_body, 0)

    b = solved_b[...]
    own = jnp.sum(gram_of(b) * eye, axis=0, keepdims=True)
    squares[col] = jnp.concatenate([own, own], axis=1)
    for x, y in col_peers:
        pltpu.make_async_remote_copy(
            src_ref=squares.at[col], dst_ref=squares.at[col], send_sem=last_send, recv_sem=last_recv,
            device_id=device_on_col(x, y), device_id_type=MESH,
        ).start()
    pltpu.make_async_copy(squares.at[pl.ds(0, 15)], squares.at[pl.ds(0, 15)], last_recv).wait()
    total = squares[0]
    for source in range(1, COLS):
        total = total + squares[source]
    scales = jnp.sqrt(total[:, :64] / cols_all + EPSILON)
    out_scales[1:2, :] = scales
    out_b[...] = b / jnp.sum(eye * scales, axis=1, keepdims=True)

    def drain(sweep, carry):
        left(grams_a.at[sweep, pl.ds(0, 15)], sweep, 0)
        left(sums_a.at[sweep, pl.ds(0, 15)], sweep, 1)
        left(full_a.at[sweep, pl.ds(0, 7)], sweep, 2)
        left(pair_g.at[sweep], sweep, 3)
        left(pair_b.at[sweep], sweep, 4)
        left(grams_b.at[sweep, pl.ds(0, 15)], sweep, 5)
        left(sums_b.at[sweep, pl.ds(0, 15)], sweep, 6)
        left(pair_g.at[sweep], sweep, 7)
        left(sums_b.at[sweep, pl.ds(0, 15)], sweep, 8)
        return carry

    lax.fori_loop(0, SWEEPS, drain, 0)
    pltpu.make_async_copy(squares.at[pl.ds(0, 15)], squares.at[pl.ds(0, 15)], last_send).wait()


def shards(tensor, factor_b, factor_c):
    vmem = pl.BlockSpec(memory_space=pltpu.VMEM)
    whole = pl.BlockSpec(memory_space=pl.ANY)
    n = SWEEPS
    return pl.pallas_call(
        kernel,
        out_shape=(
            jax.ShapeDtypeStruct((64, 256), F32),
            jax.ShapeDtypeStruct((64, 256), F32),
            jax.ShapeDtypeStruct((2, 64), F32),
        ),
        in_specs=[whole, vmem, vmem],
        out_specs=(vmem, vmem, vmem),
        scratch_shapes=[
            pltpu.VMEM((16, 256, 256), F32),
            pltpu.VMEM((16, 256, 256), BF16),
            pltpu.VMEM((16, 256, 256), BF16),
            pltpu.VMEM((16, 64, 128), F32),
            pltpu.VMEM((16, 128), F32),
            pltpu.VMEM((64, 64), F32),
            pltpu.VMEM((64, 256), F32),
            pltpu.VMEM((64, 256), F32),
            pltpu.VMEM((n, 8, 8, 256), F32),
            pltpu.VMEM((n, 16, 8, 256), F32),
            pltpu.VMEM((n, 8, 8, 256), F32),
            pltpu.VMEM((n, 16, 32, 128), F32),
            pltpu.VMEM((n, 2, 64, 128), F32),
            pltpu.VMEM((n, 64, 128), F32),
            pltpu.VMEM((n, 8, 8, 128), F32),
            pltpu.VMEM((n, 16, 8, 128), F32),
            pltpu.VMEM((n, 2, 8, 8, 128), F32),
            pltpu.VMEM((n, 2, 16, 128), F32),
            pltpu.VMEM((n, 16, 128), F32),
            pltpu.VMEM((n, 16, 16, 128), F32),
            pltpu.VMEM((n, 2, 16, 128), F32),
            pltpu.VMEM((16, 1, 128), F32),
            pltpu.SemaphoreType.DMA((16,)),
            pltpu.SemaphoreType.DMA((n, 9)),
            pltpu.SemaphoreType.DMA((n, 9)),
            pltpu.SemaphoreType.DMA,
            pltpu.SemaphoreType.DMA,
        ],
        compiler_params=pltpu.CompilerParams(collective_id=0, has_side_effects=True, vmem_limit_bytes=40 * 2**20),
        name="sweeps",
    )(tensor, factor_b, factor_c)


def solution(mesh):
    in_specs = (P(None, "row", "col"), P(None, "col"), P())
    out_specs = (P(None, "row"), P(None, "col"), P())
    return jax.shard_map(shards, mesh=mesh, in_specs=in_specs, out_specs=out_specs, check_vma=False)
```

time: 1640 us -> 124 us (0.08)
  waiting for transfers between devices: 803 us -> 0 us
  blocking collectives: 683 us -> 0 us
  Pallas kernels: 0 us -> 118 us
  other arithmetic: 74 us -> 0 us
  matrix products: 49.1 us -> 0 us
    psum x6 -> x0, waiting for transfers between devices: 803 us -> none  [the longest x3 535 us: shards(): summed_b = lax.psum(partial_b, 'row')]
    psum x12 -> x0, blocking collectives: 683 us -> none  [the longest x3 264 us: settle_left(): return (normed, scales, lax.psum(gram_of(normed), 'row'))]
    pallas_call x0 -> x1, Pallas kernels: none -> 118 us  [shards(): pl.pallas_call(kernel, out_shape=(jax.ShapeDtypeStruct((64, 256), F32), j...]
    another operation x33 -> x0, other arithmetic: 73 us -> none  [the longest x9 19.6 us: shards(): lower_a = jnp.linalg.cholesky(gram_c * gram_b + cols_all * identity)]
    dot_general x18 -> x0, matrix products: 40.9 us -> none  [the longest x3 18.1 us: shards(): inner = jnp.einsum('kij,rj->kir', tensor, current_b, precision=highest)]
  transfers between devices with their start and end apart: 6 -> 0, of which waited for: 6 -> 0; matrix products, arithmetic and copies ran while one was open for 2% -> 0% of each run, Pallas kernels for 0% -> 0%
where the time goes in v1:
time: 124 us
  Pallas kernels  118 us (95%)
  local copies, waits for them, and re-layouts  5.54 us (4%)
    pallas_call x1, Pallas kernels, shards(): pl.pallas_call(kernel, out_shape=(jax.ShapeDtypeStruct((64, 256), F32), j...  118 us
    unnamed x9, local copies, waits for them, and re-layouts  5.54 us

profile of v1, /device:TPU:1, one launch (start us, length us, event | category | flops | bytes accessed | tf_op | source)
XLA Modules:
  0.0 123.9 jit_solution(12654438772889794699)
XLA Ops:
  0.6 0.0 copy-start
  0.6 2.2 %copy-done = f32[16,256,256]{2,1,0:T(8,128)S(1)} copy-done((f32[16,256,256]{2,1,0:T(8,128)S(1)}, f32[16,256,256]{2,1,0:T(8,128)}, u32[]{:S(2)}) %copy-start) | copy-done | bytes 4194328
  2.8 0.0 copy-start.1
  2.8 0.8 copy-done.1
  3.7 0.0 copy-start.2
  3.7 0.7 copy-done.2
  4.4 117.7 %sweeps.1 = (f32[64,256]{1,0:T(8,128)S(1)}, f32[64,256]{1,0:T(8,128)S(1)}, f32[2,64]{1,0:T(2,128)S(1)}) custom-call(f32[16,256,256]{2,1,0:T(8,128)S(1)} %copy-done, f32[64,256]{1,0:T(8,128)S(1)} %copy-done.1, f32[16,64]{1,0:T(8,128)S(1)} %copy-done.2), custom_call_target="tpu_custom_call" | custom-call | tf_op jit(solution)/shard_map/sweeps/pallas_call | solution.py:300
  122.1 0.6 copy.9
  122.7 0.6 copy.10
  123.3 0.6 copy.11
Async XLA Ops:
  0.6 2.2 %copy-start = (f32[16,256,256]{2,1,0:T(8,128)S(1)}, f32[16,256,256]{2,1,0:T(8,128)}, u32[]{:S(2)}) copy-start(f32[16,256,256]{2,1,0:T(8,128)} %tensor.1) | copy-start | bytes 12582916
  2.8 0.8 copy-start.1
  3.7 0.7 copy-start.2

commit v2 on v1

--- a/solution.py
+++ b/solution.py
@@ -53,40 +53,39 @@
     rows = [work[8 * i : 8 * i + 8] for i in range(8)]
     sublane = lax.broadcasted_iota(jnp.int32, (8, 128), 0)
     for panel in range(8):
-        columns = [
-            [jnp.broadcast_to(rows[i][:, 8 * panel + k : 8 * panel + k + 1], (8, 128)) for k in range(8)]
-            for i in range(8)
-        ]
-        own = list(columns[panel])
+        lane = 8 * panel
         value = rows[panel]
+        own = [spread(value[:, lane + k : lane + k + 1]) for k in range(8)]
+        factors = []
         inverses = jnp.zeros((8, 128), F32)
         for k in range(8):
             inverse = 1.0 / spread(own[k][k : k + 1])
             inverses = jnp.where(sublane == k, inverse, inverses)
-            factor = jnp.where(sublane == k, 0.0, own[k] * inverse)
-            value = value - factor * spread(value[k : k + 1])
+            factors.append(jnp.where(sublane == k, 0.0, own[k] * inverse))
             for m in range(k + 1, 8):
-                own[m] = own[m] - factor * spread(own[m][k : k + 1])
+                own[m] = own[m] - factors[k] * spread(own[m][k : k + 1])
+        for k in range(8):
+            value = value - factors[k] * spread(value[k : k + 1])
         value = value * inverses
         rows[panel] = value
         pivots = [spread(value[k : k + 1]) for k in range(8)]
         for i in range(8):
             if i != panel:
-                total = rows[i]
-                for k in range(8):
-                    total = total - columns[i][k] * pivots[k]
-                rows[i] = total
+                terms = [spread(rows[i][:, lane + k : lane + k + 1]) * pivots[k] for k in range(8)]
+                while len(terms) > 1:
+                    terms = [x + y for x, y in zip(terms[::2], terms[1::2])]
+                rows[i] = rows[i] - terms[0]
     return jnp.concatenate(rows, axis=0)[:, 64:]
 
 
 def kernel(
     tensor, factor_b, factor_c,
     out_a, out_b, out_scales,
-    staged, high, low, wide_c, twin_c, gram_c, solved_a, solved_b,
+    staged, high, low, high_t, low_t, wide_c, twin_c, gram_c, solved_b,
     part_a, sums_a, full_a, grams_a,
     part_b, pair_b, half_b, sums_b, full_b,
-    halves_g, pair_g, grams_b, full_g, squares,
-    load_sem, send_sem, recv_sem, last_send, last_recv,
+    whole_g, halves_g, pair_g, grams_b, full_g, squares,
+    own_c, small_sem, load_sem, send_sem, recv_sem, last_send, last_recv,
 ):
     row, col = lax.axis_index("row"), lax.axis_index("col")
     chip, core = row // 2, lax.rem(row, 2)
@@ -107,6 +106,7 @@
     col_peers = [at_col(*offset) for offset in col_offsets]
     chip_offsets = sorted(range(1, CHIPS), key=lambda o: -ring(o, CHIPS))
     chip_peers = [at_chip(offset) for offset in chip_offsets]
+    x_peers = [lax.rem(col_x + dx, SIDE) for dx in (2, 1, 3)]
     share = share_of(col_x, col_y)
     tile = lax.rem(chip, 8)
 
@@ -115,6 +115,9 @@
 
     def device_on_row(z, c):
         return (z * 2 + c, col)
+
+    def device_across(x, c):
+        return (chip * 2 + c, x * SIDE + col_y)
 
     barrier = pltpu.get_barrier_semaphore()
 
@@ -127,29 +130,28 @@
         load(k).start()
         return carry
 
+    small = [
+        pltpu.make_async_copy(factor_c, own_c, small_sem.at[0]),
+        pltpu.make_async_copy(factor_b, solved_b, small_sem.at[1]),
+    ]
+    for copy in small:
+        copy.start()
     lax.fori_loop(0, chunks, start_load, 0)
 
     greeted = [device_on_col(x, y) for x, y in col_peers]
     greeted += [device_on_row(z, c) for z in chip_peers for c in (0, 1)] + [sibling]
+    greeted += [device_across(x, 1 - core) for x in x_peers]
     for device in greeted:
         pl.semaphore_signal(barrier, inc=1, device_id=device, device_id_type=MESH)
 
-    c = factor_c[...]
+    small[0].wait()
+    c = own_c[...]
     gram_c[...] = lax.dot_general(c, c, (((0,), (0,)), ((), ())), precision=HIGHEST, preferred_element_type=F32)
     twin_c[...] = jnp.concatenate([c, c], axis=1)
     c_columns = c.T
     for k in range(chunks):
         wide_c[k] = jnp.broadcast_to(c_columns[:, k : k + 1], (64, 128))
-    solved_b[...] = factor_b[...]
-
-    def take(k, carry):
-        load(k).wait()
-        first, second = halves(staged[k])
-        high[k] = first
-        low[k] = second
-        return carry
-
-    lax.fori_loop(0, chunks, take, 0)
+    small[1].wait()
 
     eye = jnp.where(
         lax.broadcasted_iota(jnp.int32, (64, 64), 0) == lax.broadcasted_iota(jnp.int32, (64, 64), 1), 1.0, 0.0
@@ -181,29 +183,64 @@
             total = total + ref[sweep, source]
         return total
 
+    def mttkrp(factor, first, second):
+        total = jnp.zeros((128, 256), F32)
+        for k in range(chunks):
+            weights = stacked(jnp.concatenate([wide_c[k], wide_c[k]], axis=1) * factor)
+            total = total + jnp.dot(weights, first[k], preferred_element_type=F32)
+            total = total + jnp.dot(weights, second[k], preferred_element_type=F32)
+        return total[:64] + total[64:]
+
+    def keep_gram_a(sweep, b):
+        pack = packed(gram_of(b))
+        grams_a[sweep, col] = jnp.where(core == 0, pack[:16], pack[16:])
+
+    b = solved_b[...]
+    weights_b = stacked(b)
+
+    def take(group, total):
+        for i in range(4):
+            load(4 * group + i).wait()
+        for i in range(4):
+            k = 4 * group + i
+            first, second = halves(staged[k])
+            high[k] = first
+            low[k] = second
+            part = lax.dot_general(first, weights_b, (((1,), (1,)), ((), ())), preferred_element_type=F32)
+            part = part + lax.dot_general(second, weights_b, (((1,), (1,)), ((), ())), preferred_element_type=F32)
+            total = total + part * twin_c[pl.ds(k, 1), :]
+        return total
+
+    total = lax.fori_loop(0, chunks // 4, take, jnp.zeros((256, 128), F32))
+    part_a[0] = (total[:, :64] + total[:, 64:]).T.reshape(8, 8, 256)
+    keep_gram_a(0, b)
     pl.semaphore_wait(barrier, len(greeted))
 
+    def turn(k, carry):
+        high_t[k] = high[k].T
+        low_t[k] = low[k].T
+        return carry
+
     def sweep_body(sweep, carry):
-        b = solved_b[...]
-        grams_a[sweep, col] = packed(gram_of(b))
+        for x, y in col_peers:
+            send(part_a.at[sweep, share_of(x, y)], sums_a.at[sweep, col], sweep, 1, device_on_col(x, y))
         for x, y in col_peers:
             send(grams_a.at[sweep, col], grams_a.at[sweep, col], sweep, 0, device_on_col(x, y))
-        weights = stacked(b)
-        total = jnp.zeros((256, 128), F32)
-        for k in range(chunks):
-            part = lax.dot_general(high[k], weights, (((1,), (1,)), ((), ())), preferred_element_type=F32)
-            part = part + lax.dot_general(low[k], weights, (((1,), (1,)), ((), ())), preferred_element_type=F32)
-            total = total + part * twin_c[k : k + 1, :]
-        part_a[sweep] = (total[:, :64] + total[:, 64:]).T.reshape(8, 8, 256)
-        for x, y in col_peers:
-            send(part_a.at[sweep, share_of(x, y)], sums_a.at[sweep, col], sweep, 1, device_on_col(x, y))
         sums_a[sweep, col] = part_a[sweep, share]
+
+        @pl.when(sweep == 0)
+        def _():
+            lax.fori_loop(0, chunks, turn, 0)
+
         arrived(sums_a.at[sweep, pl.ds(0, 15)], sweep, 1)
         full_a[sweep, share] = added(sums_a, sweep)
         for offset in SERVED[1:]:
             send(full_a.at[sweep, share], full_a.at[sweep, share], sweep, 2, device_on_col(*at_col(*offset)))
         arrived(grams_a.at[sweep, pl.ds(0, 15)], sweep, 0)
-        gram = unpacked(added(grams_a, sweep))
+        whole_g[sweep, core] = added(grams_a, sweep)
+        send(whole_g.at[sweep, core], whole_g.at[sweep, core], sweep, 9, sibling)
+        arrived(whole_g.at[sweep, 0], sweep, 9)
+        gram = unpacked(whole_g[sweep].reshape(32, 128))
         given = sweep == 0
         across = jnp.where(given, 1.0, 1.0 / scales_row(gram, cols_all))
         down = jnp.where(given, 1.0, 1.0 / scales_column(gram, cols_all))
@@ -211,22 +248,19 @@
         solver = eliminate(jnp.concatenate([system, eye * across], axis=1))
         arrived(full_a.at[sweep, pl.ds(0, 7)], sweep, 2)
         a = jnp.dot(solver, full_a[sweep].reshape(64, 256), precision=HIGHEST, preferred_element_type=F32)
-        solved_a[...] = a
-
-        halves_g[sweep] = packed(gram_of(a)).reshape(2, 16, 128)
-        send(halves_g.at[sweep, 1 - core], pair_g.at[sweep], sweep, 3, sibling)
-        total = jnp.zeros((128, 256), F32)
-        for k in range(chunks):
-            scaled = jnp.concatenate([wide_c[k], wide_c[k]], axis=1) * a
-            weights = stacked(scaled)
-            total = total + jnp.dot(weights, high[k], preferred_element_type=F32)
-            total = total + jnp.dot(weights, low[k], preferred_element_type=F32)
-        total = total[:64] + total[64:]
+
+        pack = packed(gram_of(a))
+        for half in range(2):
+            for x in range(SIDE):
+                at = 16 * half + 4 * x
+                halves_g[sweep, half, x] = pack[at : at + 4]
+        send(halves_g.at[sweep, 1 - core, col_x], pair_g.at[sweep], sweep, 3, sibling)
+        total = mttkrp(a, high, low)
         part_b[sweep, 0] = total[:, :128]
         part_b[sweep, 1] = total[:, 128:]
         send(part_b.at[sweep, 1 - core], pair_b.at[sweep], sweep, 4, sibling)
         arrived(pair_g.at[sweep], sweep, 3)
-        grams_b[sweep, chip] = halves_g[sweep, core] + pair_g[sweep]
+        grams_b[sweep, chip] = halves_g[sweep, core, col_x] + pair_g[sweep]
         for z in chip_peers:
             send(grams_b.at[sweep, chip], grams_b.at[sweep, chip], sweep, 5, device_on_row(z, core))
         arrived(pair_b.at[sweep], sweep, 4)
@@ -235,18 +269,22 @@
             send(half_b.at[sweep, lax.rem(z, 8)], sums_b.at[sweep, chip], sweep, 6, device_on_row(z, core))
         sums_b[sweep, chip] = half_b[sweep, tile]
         arrived(grams_b.at[sweep, pl.ds(0, 15)], sweep, 5)
-        full_g[sweep, core] = added(grams_b, sweep)
-        send(full_g.at[sweep, core], full_g.at[sweep, core], sweep, 7, sibling)
+        full_g[sweep, core, col_x] = added(grams_b, sweep)
+        piece = full_g.at[sweep, core, col_x]
+        for x in x_peers:
+            for c in (0, 1):
+                send(piece, piece, sweep, 7, device_across(x, c))
+        send(piece, piece, sweep, 7, sibling)
         arrived(sums_b.at[sweep, pl.ds(0, 15)], sweep, 6)
         full_b[sweep, core, tile] = added(sums_b, sweep)
         for offset in WINDOW:
-            z = at_chip(offset)
+            z = at_chip(offset * (1 - 2 * core))
             own = full_b.at[sweep, core, tile]
             send(own, own, sweep, 8, device_on_row(z, 1 - core))
             if offset:
                 send(own, own, sweep, 8, device_on_row(z, core))
-        arrived(pair_g.at[sweep], sweep, 7)
-        gram = unpacked(full_g[sweep].reshape(32, 128))
+        arrived(grams_b.at[sweep, pl.ds(0, 7)], sweep, 7)
+        gram = unpacked(jnp.concatenate([full_g[sweep, half, x] for half in range(2) for x in range(SIDE)], axis=0))
         scales = scales_row(gram, rows_all)
         out_scales[0:1, :] = scales
         across = 1.0 / scales
@@ -256,7 +294,17 @@
         solver = eliminate(jnp.concatenate([system, eye * across], axis=1))
         arrived(sums_b.at[sweep, pl.ds(0, 15)], sweep, 8)
         summed = jnp.concatenate([full_b[sweep, 0].reshape(64, 128), full_b[sweep, 1].reshape(64, 128)], axis=1)
-        solved_b[...] = jnp.dot(solver, summed, precision=HIGHEST, preferred_element_type=F32)
+
+        @pl.when(sweep < SWEEPS - 1)
+        def _():
+            b = jnp.dot(solver, summed, precision=HIGHEST, preferred_element_type=F32)
+            part_a[sweep + 1] = mttkrp(b, high_t, low_t).reshape(8, 8, 256)
+            keep_gram_a(sweep + 1, b)
+
+        @pl.when(sweep == SWEEPS - 1)
+        def _():
+            solved_b[...] = jnp.dot(solver, summed, precision=HIGHEST, preferred_element_type=F32)
+
         return carry
 
     lax.fori_loop(0, SWEEPS, sweep_body, 0)
@@ -285,59 +333,79 @@
         left(pair_b.at[sweep], sweep, 4)
         left(grams_b.at[sweep, pl.ds(0, 15)], sweep, 5)
         left(sums_b.at[sweep, pl.ds(0, 15)], sweep, 6)
-        left(pair_g.at[sweep], sweep, 7)
+        left(grams_b.at[sweep, pl.ds(0, 7)], sweep, 7)
         left(sums_b.at[sweep, pl.ds(0, 15)], sweep, 8)
+        left(whole_g.at[sweep, 0], sweep, 9)
         return carry
 
     lax.fori_loop(0, SWEEPS, drain, 0)
     pltpu.make_async_copy(squares.at[pl.ds(0, 15)], squares.at[pl.ds(0, 15)], last_send).wait()
+
+
+def place(a, b, scales, out_a, out_b, out_scales):
+    out_a[...] = a[...]
+    out_b[...] = b[...]
+    out_scales[...] = scales[...]
 
 
 def shards(tensor, factor_b, factor_c):
     vmem = pl.BlockSpec(memory_space=pltpu.VMEM)
     whole = pl.BlockSpec(memory_space=pl.ANY)
     n = SWEEPS
-    return pl.pallas_call(
+    outs = (
+        jax.ShapeDtypeStruct((64, 256), F32),
+        jax.ShapeDtypeStruct((64, 256), F32),
+        jax.ShapeDtypeStruct((2, 64), F32),
+    )
+    results = pl.pallas_call(
         kernel,
-        out_shape=(
-            jax.ShapeDtypeStruct((64, 256), F32),
-            jax.ShapeDtypeStruct((64, 256), F32),
-            jax.ShapeDtypeStruct((2, 64), F32),
-        ),
-        in_specs=[whole, vmem, vmem],
+        out_shape=outs,
+        in_specs=[whole, whole, whole],
         out_specs=(vmem, vmem, vmem),
         scratch_shapes=[
             pltpu.VMEM((16, 256, 256), F32),
+            pltpu.VMEM((16, 256, 256), BF16),
+            pltpu.VMEM((16, 256, 256), BF16),
             pltpu.VMEM((16, 256, 256), BF16),
             pltpu.VMEM((16, 256, 256), BF16),
             pltpu.VMEM((16, 64, 128), F32),
             pltpu.VMEM((16, 128), F32),
             pltpu.VMEM((64, 64), F32),
             pltpu.VMEM((64, 256), F32),
-            pltpu.VMEM((64, 256), F32),
             pltpu.VMEM((n, 8, 8, 256), F32),
             pltpu.VMEM((n, 16, 8, 256), F32),
             pltpu.VMEM((n, 8, 8, 256), F32),
-            pltpu.VMEM((n, 16, 32, 128), F32),
+            pltpu.VMEM((n, 16, 16, 128), F32),
             pltpu.VMEM((n, 2, 64, 128), F32),
             pltpu.VMEM((n, 64, 128), F32),
             pltpu.VMEM((n, 8, 8, 128), F32),
             pltpu.VMEM((n, 16, 8, 128), F32),
             pltpu.VMEM((n, 2, 8, 8, 128), F32),
             pltpu.VMEM((n, 2, 16, 128), F32),
-            pltpu.VMEM((n, 16, 128), F32),
-            pltpu.VMEM((n, 16, 16, 128), F32),
-            pltpu.VMEM((n, 2, 16, 128), F32),
+            pltpu.VMEM((n, 2, 4, 4, 128), F32),
+            pltpu.VMEM((n, 4, 128), F32),
+            pltpu.VMEM((n, 16, 4, 128), F32),
+            pltpu.VMEM((n, 2, 4, 4, 128), F32),
             pltpu.VMEM((16, 1, 128), F32),
+            pltpu.VMEM((16, 64), F32),
+            pltpu.SemaphoreType.DMA((2,)),
             pltpu.SemaphoreType.DMA((16,)),
-            pltpu.SemaphoreType.DMA((n, 9)),
-            pltpu.SemaphoreType.DMA((n, 9)),
+            pltpu.SemaphoreType.DMA((n, 10)),
+            pltpu.SemaphoreType.DMA((n, 10)),
             pltpu.SemaphoreType.DMA,
             pltpu.SemaphoreType.DMA,
         ],
-        compiler_params=pltpu.CompilerParams(collective_id=0, has_side_effects=True, vmem_limit_bytes=40 * 2**20),
+        compiler_params=pltpu.CompilerParams(collective_id=0, has_side_effects=True, vmem_limit_bytes=54 * 2**20),
         name="sweeps",
     )(tensor, factor_b, factor_c)
+    return pl.pallas_call(
+        place,
+        out_shape=outs,
+        in_specs=[vmem] * 3,
+        out_specs=(vmem, vmem, vmem),
+        compiler_params=pltpu.CompilerParams(vmem_limit_bytes=54 * 2**20),
+        name="place",
+    )(*results)
 
 
 def solution(mesh):

time: 124 us -> 102 us (0.82)
  Pallas kernels: 118 us -> 101 us
  local copies, waits for them, and re-layouts: 5.54 us -> 0 us
    pallas_call x1 -> x2, Pallas kernels: 118 us -> 101 us  [the longest x1 99.3 us: shards(): pl.pallas_call(kernel, out_shape=outs, in_specs=[whole, whole, whole], ou...]
    unnamed x9 -> x0, local copies, waits for them, and re-layouts: 5.54 us -> none
where the time goes in v2:
time: 102 us; the launch traced here: 101 us
  Pallas kernels  101 us (99%)
    pallas_call x1, Pallas kernels, shards(): pl.pallas_call(kernel, out_shape=outs, in_specs=[whole, whole, whole], ou...  99.3 us

profile of v2, /device:TPU:1, one launch (start us, length us, event | category | flops | bytes accessed | tf_op | source)
XLA Modules:
  0.0 101.5 jit_solution(5555096003368666723)
XLA Ops:
  0.6 99.3 %sweeps.1 = (f32[64,256]{1,0:T(8,128)}, f32[64,256]{1,0:T(8,128)}, f32[2,64]{1,0:T(2,128)}) custom-call(f32[16,256,256]{2,1,0:T(8,128)} %tensor.1, f32[64,256]{1,0:T(8,128)} %factor_b.1, f32[16,64]{1,0:T(8,128)} %factor_c.1), custom_call_target="tpu_custom_call" | custom-call | tf_op jit(solution)/shard_map/sweeps/pallas_call | solution.py:360
  99.9 1.5 %place.1 = (f32[64,256]{1,0:T(8,128)}, f32[64,256]{1,0:T(8,128)}, f32[2,64]{1,0:T(2,128)}) custom-call(f32[64,256]{1,0:T(8,128)} %get-tuple-element.6.a, f32[64,256]{1,0:T(8,128)} %get-tuple-element.7.b, f32[2,64]{1,0:T(2,128)} %get-tuple-element.8.scales), custom_call_target="tpu_custom_call" | custom-call | tf_op jit(solution)/shard_map/place/pallas_call | solution.py:401

commit v3 on v2

--- a/solution.py
+++ b/solution.py
@@ -16,7 +16,6 @@
 COLS = 16
 SIDE = 4
 
-SERVED = ((0, 0), (1, 0), (3, 0), (0, 1), (0, 3), (2, 0), (1, 1), (1, 3))
 WINDOW = (-4, -3, 3, -2, 2, -1, 1, 0)
 
 
@@ -84,7 +83,7 @@
     staged, high, low, high_t, low_t, wide_c, twin_c, gram_c, solved_b,
     part_a, sums_a, full_a, grams_a,
     part_b, pair_b, half_b, sums_b, full_b,
-    whole_g, halves_g, pair_g, grams_b, full_g, squares,
+    whole_g, pieces_g, grams_b, full_g, squares,
     own_c, small_sem, load_sem, send_sem, recv_sem, last_send, last_recv,
 ):
     row, col = lax.axis_index("row"), lax.axis_index("col")
@@ -95,9 +94,6 @@
     def at_col(dx, dy):
         return lax.rem(col_x + dx, SIDE), lax.rem(col_y + dy, SIDE)
 
-    def share_of(x, y):
-        return lax.rem(x, 2) * SIDE + lax.rem(y + 2 * (x // 2), SIDE)
-
     def at_chip(offset):
         return lax.rem(chip + offset + CHIPS, CHIPS)
 
@@ -106,8 +102,6 @@
     col_peers = [at_col(*offset) for offset in col_offsets]
     chip_offsets = sorted(range(1, CHIPS), key=lambda o: -ring(o, CHIPS))
     chip_peers = [at_chip(offset) for offset in chip_offsets]
-    x_peers = [lax.rem(col_x + dx, SIDE) for dx in (2, 1, 3)]
-    share = share_of(col_x, col_y)
     tile = lax.rem(chip, 8)
 
     def device_on_col(x, y):
@@ -116,10 +110,16 @@
     def device_on_row(z, c):
         return (z * 2 + c, col)
 
-    def device_across(x, c):
-        return (chip * 2 + c, x * SIDE + col_y)
+    def device_across(x, y, c):
+        return (chip * 2 + c, x * SIDE + y)
 
     barrier = pltpu.get_barrier_semaphore()
+    greeted = [device_on_row(z, core) for z in chip_peers]
+    greeted += [device_on_row(at_chip(offset * (1 - 2 * core)), 1 - core) for offset in WINDOW]
+    greeted += [device_on_col(x, y) for x, y in col_peers]
+    greeted += [device_across(x, y, 1 - core) for x, y in col_peers]
+    for device in greeted[:15]:
+        pl.semaphore_signal(barrier, inc=1, device_id=device, device_id_type=MESH)
 
     chunks = tensor.shape[0]
 
@@ -137,11 +137,7 @@
     for copy in small:
         copy.start()
     lax.fori_loop(0, chunks, start_load, 0)
-
-    greeted = [device_on_col(x, y) for x, y in col_peers]
-    greeted += [device_on_row(z, c) for z in chip_peers for c in (0, 1)] + [sibling]
-    greeted += [device_across(x, 1 - core) for x in x_peers]
-    for device in greeted:
+    for device in greeted[15:]:
         pl.semaphore_signal(barrier, inc=1, device_id=device, device_id_type=MESH)
 
     small[0].wait()
@@ -190,6 +186,10 @@
             total = total + jnp.dot(weights, first[k], preferred_element_type=F32)
             total = total + jnp.dot(weights, second[k], preferred_element_type=F32)
         return total[:64] + total[64:]
+
+    def keep_part_a(sweep, part):
+        part_a[sweep, 0:8] = part[:, :128].reshape(8, 8, 128)
+        part_a[sweep, 8:16] = part[:, 128:].reshape(8, 8, 128)
 
     def keep_gram_a(sweep, b):
         pack = packed(gram_of(b))
@@ -212,7 +212,7 @@
         return total
 
     total = lax.fori_loop(0, chunks // 4, take, jnp.zeros((256, 128), F32))
-    part_a[0] = (total[:, :64] + total[:, 64:]).T.reshape(8, 8, 256)
+    keep_part_a(0, (total[:, :64] + total[:, 64:]).T)
     keep_gram_a(0, b)
     pl.semaphore_wait(barrier, len(greeted))
 
@@ -223,19 +223,19 @@
 
     def sweep_body(sweep, carry):
         for x, y in col_peers:
-            send(part_a.at[sweep, share_of(x, y)], sums_a.at[sweep, col], sweep, 1, device_on_col(x, y))
+            send(part_a.at[sweep, x * SIDE + y], sums_a.at[sweep, col], sweep, 1, device_on_col(x, y))
         for x, y in col_peers:
             send(grams_a.at[sweep, col], grams_a.at[sweep, col], sweep, 0, device_on_col(x, y))
-        sums_a[sweep, col] = part_a[sweep, share]
+        sums_a[sweep, col] = part_a[sweep, col]
 
         @pl.when(sweep == 0)
         def _():
             lax.fori_loop(0, chunks, turn, 0)
 
         arrived(sums_a.at[sweep, pl.ds(0, 15)], sweep, 1)
-        full_a[sweep, share] = added(sums_a, sweep)
-        for offset in SERVED[1:]:
-            send(full_a.at[sweep, share], full_a.at[sweep, share], sweep, 2, device_on_col(*at_col(*offset)))
+        full_a[sweep, col] = added(sums_a, sweep)
+        for x, y in col_peers:
+            send(full_a.at[sweep, col], full_a.at[sweep, col], sweep, 2, device_on_col(x, y))
         arrived(grams_a.at[sweep, pl.ds(0, 15)], sweep, 0)
         whole_g[sweep, core] = added(grams_a, sweep)
         send(whole_g.at[sweep, core], whole_g.at[sweep, core], sweep, 9, sibling)
@@ -246,34 +246,31 @@
         down = jnp.where(given, 1.0, 1.0 / scales_column(gram, cols_all))
         system = gram_c[...] * (gram * down * across) + cols_all * eye
         solver = eliminate(jnp.concatenate([system, eye * across], axis=1))
-        arrived(full_a.at[sweep, pl.ds(0, 7)], sweep, 2)
-        a = jnp.dot(solver, full_a[sweep].reshape(64, 256), precision=HIGHEST, preferred_element_type=F32)
+        arrived(full_a.at[sweep, pl.ds(0, 15)], sweep, 2)
+        summed = jnp.concatenate([full_a[sweep, 0:8].reshape(64, 128), full_a[sweep, 8:16].reshape(64, 128)], axis=1)
+        a = jnp.dot(solver, summed, precision=HIGHEST, preferred_element_type=F32)
 
         pack = packed(gram_of(a))
-        for half in range(2):
-            for x in range(SIDE):
-                at = 16 * half + 4 * x
-                halves_g[sweep, half, x] = pack[at : at + 4]
-        send(halves_g.at[sweep, 1 - core, col_x], pair_g.at[sweep], sweep, 3, sibling)
+        for i in range(COLS):
+            pieces_g[sweep, i] = pack[2 * i : 2 * i + 2]
+        grams_b[sweep, chip] = pieces_g[sweep, col]
+        for z in chip_peers:
+            send(grams_b.at[sweep, chip], grams_b.at[sweep, chip], sweep, 5, device_on_row(z, core))
         total = mttkrp(a, high, low)
         part_b[sweep, 0] = total[:, :128]
         part_b[sweep, 1] = total[:, 128:]
         send(part_b.at[sweep, 1 - core], pair_b.at[sweep], sweep, 4, sibling)
-        arrived(pair_g.at[sweep], sweep, 3)
-        grams_b[sweep, chip] = halves_g[sweep, core, col_x] + pair_g[sweep]
-        for z in chip_peers:
-            send(grams_b.at[sweep, chip], grams_b.at[sweep, chip], sweep, 5, device_on_row(z, core))
         arrived(pair_b.at[sweep], sweep, 4)
         half_b[sweep] = (part_b[sweep, core] + pair_b[sweep]).reshape(8, 8, 128)
         for z in chip_peers:
             send(half_b.at[sweep, lax.rem(z, 8)], sums_b.at[sweep, chip], sweep, 6, device_on_row(z, core))
         sums_b[sweep, chip] = half_b[sweep, tile]
         arrived(grams_b.at[sweep, pl.ds(0, 15)], sweep, 5)
-        full_g[sweep, core, col_x] = added(grams_b, sweep)
-        piece = full_g.at[sweep, core, col_x]
-        for x in x_peers:
+        full_g[sweep, core * COLS + col] = added(grams_b, sweep)
+        piece = full_g.at[sweep, core * COLS + col]
+        for x, y in col_peers:
             for c in (0, 1):
-                send(piece, piece, sweep, 7, device_across(x, c))
+                send(piece, piece, sweep, 7, device_across(x, y, c))
         send(piece, piece, sweep, 7, sibling)
         arrived(sums_b.at[sweep, pl.ds(0, 15)], sweep, 6)
         full_b[sweep, core, tile] = added(sums_b, sweep)
@@ -283,13 +280,18 @@
             send(own, own, sweep, 8, device_on_row(z, 1 - core))
             if offset:
                 send(own, own, sweep, 8, device_on_row(z, core))
-        arrived(grams_b.at[sweep, pl.ds(0, 7)], sweep, 7)
-        gram = unpacked(jnp.concatenate([full_g[sweep, half, x] for half in range(2) for x in range(SIDE)], axis=0))
+        arrived(full_g.at[sweep, pl.ds(0, 31)], sweep, 7)
+        pack = jnp.concatenate([full_g[sweep, i] + full_g[sweep, COLS + i] for i in range(COLS)], axis=0)
+        gram = unpacked(pack)
         scales = scales_row(gram, rows_all)
-        out_scales[0:1, :] = scales
         across = 1.0 / scales
         down = 1.0 / scales_column(gram, rows_all)
-        out_a[...] = a * down
+
+        @pl.when(sweep == SWEEPS - 1)
+        def _():
+            out_scales[0:1, :] = scales
+            out_a[...] = a * down
+
         system = gram_c[...] * (gram * down * across) + rows_all * eye
         solver = eliminate(jnp.concatenate([system, eye * across], axis=1))
         arrived(sums_b.at[sweep, pl.ds(0, 15)], sweep, 8)
@@ -298,7 +300,7 @@
         @pl.when(sweep < SWEEPS - 1)
         def _():
             b = jnp.dot(solver, summed, precision=HIGHEST, preferred_element_type=F32)
-            part_a[sweep + 1] = mttkrp(b, high_t, low_t).reshape(8, 8, 256)
+            keep_part_a(sweep + 1, mttkrp(b, high_t, low_t))
             keep_gram_a(sweep + 1, b)
 
         @pl.when(sweep == SWEEPS - 1)
@@ -328,12 +330,11 @@
     def drain(sweep, carry):
         left(grams_a.at[sweep, pl.ds(0, 15)], sweep, 0)
         left(sums_a.at[sweep, pl.ds(0, 15)], sweep, 1)
-        left(full_a.at[sweep, pl.ds(0, 7)], sweep, 2)
-        left(pair_g.at[sweep], sweep, 3)
+        left(full_a.at[sweep, pl.ds(0, 15)], sweep, 2)
         left(pair_b.at[sweep], sweep, 4)
         left(grams_b.at[sweep, pl.ds(0, 15)], sweep, 5)
         left(sums_b.at[sweep, pl.ds(0, 15)], sweep, 6)
-        left(grams_b.at[sweep, pl.ds(0, 7)], sweep, 7)
+        left(full_g.at[sweep, pl.ds(0, 31)], sweep, 7)
         left(sums_b.at[sweep, pl.ds(0, 15)], sweep, 8)
         left(whole_g.at[sweep, 0], sweep, 9)
         return carry
@@ -372,9 +373,9 @@
             pltpu.VMEM((16, 128), F32),
             pltpu.VMEM((64, 64), F32),
             pltpu.VMEM((64, 256), F32),
-            pltpu.VMEM((n, 8, 8, 256), F32),
-            pltpu.VMEM((n, 16, 8, 256), F32),
-            pltpu.VMEM((n, 8, 8, 256), F32),
+            pltpu.VMEM((n, 16, 8, 128), F32),
+            pltpu.VMEM((n, 16, 8, 128), F32),
+            pltpu.VMEM((n, 16, 8, 128), F32),
             pltpu.VMEM((n, 16, 16, 128), F32),
             pltpu.VMEM((n, 2, 64, 128), F32),
             pltpu.VMEM((n, 64, 128), F32),
@@ -382,10 +383,9 @@
             pltpu.VMEM((n, 16, 8, 128), F32),
             pltpu.VMEM((n, 2, 8, 8, 128), F32),
             pltpu.VMEM((n, 2, 16, 128), F32),
-            pltpu.VMEM((n, 2, 4, 4, 128), F32),
-            pltpu.VMEM((n, 4, 128), F32),
-            pltpu.VMEM((n, 16, 4, 128), F32),
-            pltpu.VMEM((n, 2, 4, 4, 128), F32),
+            pltpu.VMEM((n, 16, 2, 128), F32),
+            pltpu.VMEM((n, 16, 2, 128), F32),
+            pltpu.VMEM((n, 32, 2, 128), F32),
             pltpu.VMEM((16, 1, 128), F32),
             pltpu.VMEM((16, 64), F32),
             pltpu.SemaphoreType.DMA((2,)),

time: 102 us -> 97 us (0.951)
  Pallas kernels: 101 us -> 96.1 us
    pallas_call x1, Pallas kernels: 99.3 us -> 94.6 us  [shards(): pl.pallas_call(kernel, out_shape=outs, in_specs=[whole, whole, whole], ou...]
where the time goes in v3:
time: 97 us; the launch traced here: 96.8 us
  Pallas kernels  96.1 us (99%)
    pallas_call x1, Pallas kernels, shards(): pl.pallas_call(kernel, out_shape=outs, in_specs=[whole, whole, whole], ou...  94.6 us

profile of v3, /device:TPU:1, one launch (start us, length us, event | category | flops | bytes accessed | tf_op | source)
XLA Modules:
  0.0 96.8 jit_solution(118904799269271014)
XLA Ops:
  0.6 94.6 %sweeps.1 = (f32[64,256]{1,0:T(8,128)}, f32[64,256]{1,0:T(8,128)}, f32[2,64]{1,0:T(2,128)}) custom-call(f32[16,256,256]{2,1,0:T(8,128)} %tensor.1, f32[64,256]{1,0:T(8,128)} %factor_b.1, f32[16,64]{1,0:T(8,128)} %factor_c.1), custom_call_target="tpu_custom_call" | custom-call | tf_op jit(solution)/shard_map/sweeps/pallas_call | solution.py:361
  95.3 1.5 %place.1 = (f32[64,256]{1,0:T(8,128)}, f32[64,256]{1,0:T(8,128)}, f32[2,64]{1,0:T(2,128)}) custom-call(f32[64,256]{1,0:T(8,128)} %get-tuple-element.6.a, f32[64,256]{1,0:T(8,128)} %get-tuple-element.7.b, f32[2,64]{1,0:T(2,128)} %get-tuple-element.8.scales), custom_call_target="tpu_custom_call" | custom-call | tf_op jit(solution)/shard_map/place/pallas_call | solution.py:401

commit v4 on v3

--- a/solution.py
+++ b/solution.py
@@ -55,17 +55,21 @@
         lane = 8 * panel
         value = rows[panel]
         own = [spread(value[:, lane + k : lane + k + 1]) for k in range(8)]
-        factors = []
-        inverses = jnp.zeros((8, 128), F32)
-        for k in range(8):
-            inverse = 1.0 / spread(own[k][k : k + 1])
-            inverses = jnp.where(sublane == k, inverse, inverses)
-            factors.append(jnp.where(sublane == k, 0.0, own[k] * inverse))
-            for m in range(k + 1, 8):
-                own[m] = own[m] - factors[k] * spread(own[m][k : k + 1])
-        for k in range(8):
-            value = value - factors[k] * spread(value[k : k + 1])
-        value = value * inverses
+        blocks = []
+        for k in range(0, 8, 2):
+            first, second = own[k], own[k + 1]
+            p, q = spread(first[k : k + 1]), spread(second[k : k + 1])
+            r, s = spread(first[k + 1 : k + 2]), spread(second[k + 1 : k + 2])
+            inverse = 1.0 / (p * s - q * r)
+            upper, lower = sublane == k, sublane == k + 1
+            one = jnp.where(upper, -s, jnp.where(lower, r, first * s - second * r)) * inverse
+            two = jnp.where(upper, q, jnp.where(lower, -p, second * p - first * q)) * inverse
+            keep = jnp.where(upper | lower, 0.0, 1.0)
+            blocks.append((one, two, keep))
+            for m in range(k + 2, 8):
+                own[m] = own[m] * keep - one * spread(own[m][k : k + 1]) - two * spread(own[m][k + 1 : k + 2])
+        for k, (one, two, keep) in zip(range(0, 8, 2), blocks):
+            value = value * keep - one * spread(value[k : k + 1]) - two * spread(value[k + 1 : k + 2])
         rows[panel] = value
         pivots = [spread(value[k : k + 1]) for k in range(8)]
         for i in range(8):
@@ -101,7 +105,7 @@
     col_offsets.sort(key=lambda o: -ring(o[0], SIDE) - ring(o[1], SIDE))
     col_peers = [at_col(*offset) for offset in col_offsets]
     chip_offsets = sorted(range(1, CHIPS), key=lambda o: -ring(o, CHIPS))
-    chip_peers = [at_chip(offset) for offset in chip_offsets]
+    chip_peers = [at_chip(offset * (1 - 2 * core)) for offset in chip_offsets]
     tile = lax.rem(chip, 8)
 
     def device_on_col(x, y):

time: 97 us -> 96.9 us (level)
  no operation moved by 1% of the time
where the time goes in v4:
time: 96.9 us; the launch traced here: 96.7 us
  Pallas kernels  96.1 us (99%)
    pallas_call x1, Pallas kernels, shards(): pl.pallas_call(kernel, out_shape=outs, in_specs=[whole, whole, whole], ou...  94.5 us

profile of v4, /device:TPU:1, one launch (start us, length us, event | category | flops | bytes accessed | tf_op | source)
XLA Modules:
  0.0 96.7 jit_solution(7319194652629668329)
XLA Ops:
  0.6 94.5 %sweeps.1 = (f32[64,256]{1,0:T(8,128)}, f32[64,256]{1,0:T(8,128)}, f32[2,64]{1,0:T(2,128)}) custom-call(f32[16,256,256]{2,1,0:T(8,128)} %tensor.1, f32[64,256]{1,0:T(8,128)} %factor_b.1, f32[16,64]{1,0:T(8,128)} %factor_c.1), custom_call_target="tpu_custom_call" | custom-call | tf_op jit(solution)/shard_map/sweeps/pallas_call | solution.py:365
  95.2 1.5 %place.1 = (f32[64,256]{1,0:T(8,128)}, f32[64,256]{1,0:T(8,128)}, f32[2,64]{1,0:T(2,128)}) custom-call(f32[64,256]{1,0:T(8,128)} %get-tuple-element.6.a, f32[64,256]{1,0:T(8,128)} %get-tuple-element.7.b, f32[2,64]{1,0:T(2,128)} %get-tuple-element.8.scales), custom_call_target="tpu_custom_call" | custom-call | tf_op jit(solution)/shard_map/place/pallas_call | solution.py:405
